TPU v7x, 256 devices: a whole 4x4x8 slice. The times are simulated.
256 devices in a mesh: sx: 32 (over x_lo, z, core), sy: 8 (over y, x_hi).
Axes of the slice: x: 4 (x_hi: 2, x_lo: 2; x = x_hi * 2 + x_lo), y: 4, z: 8, core: 2. Of those that a mesh axis runs over, the one named last changes fastest.
Arguments:
- field: float32 [2, 16, 128, 64, 1024], P(None, None, 'sx', 'sy'), may hold values from -6 to 6
- grad_out: float32 [2, 16, 128, 64, 1024], P(None, None, 'sx', 'sy'), may hold values from -6 to 6
- local_weight: float32 [16, 16], replicated, may hold values from -1.5 to 1.5
- mode_weight: float32 [2, 16, 16, 32768], P(None, None, None, ('sx', 'sy')), may hold values from -1 to 1
- mode_x: int32 [16], replicated, may hold values from 0 to 127, as said below
- mode_y: int32 [16], replicated, may hold values from 0 to 63, as said below
- mode_z: int32 [16], replicated, may hold values from 0 to 63, as said below
- mode_t: int32 [8], replicated, may hold values from 0 to 15, as said below
Outputs:
- grad_input: float32 [2, 16, 128, 64, 1024], P(None, None, 'sx', 'sy')
- grad_modes: float32 [2, 16, 16, 32768], P(None, None, None, ('sx', 'sy'))
Inputs may be any that keep to these rules, and one draw needn't show every extreme that they name: `mode_x`: the 16 entries are distinct. `mode_y`: the 16 entries are distinct. `mode_z`: the 16 entries are distinct. `mode_t`: the 8 entries are distinct.
All inputs are finite; a program needn't handle non-finite values.
Results may differ from a plain program's by a relative error of at most 0.00011.
Values sent between devices are 32-bit elements; how exact they have to be, the bound alone decides.
A program may use at most 128 MiB of HBM per device.

v0:
```python
import math

import jax
import jax.numpy as jnp
from jax import lax
from jax.sharding import PartitionSpec as P

NZ = 64
NT = 16


HIGH = lax.Precision.HIGHEST


def gelu_slope(values):
    normal_cdf = 0.5 * (1.0 + jax.scipy.special.erf(values * (1.0 / math.sqrt(2.0))))
    density = jnp.exp(-0.5 * values * values) * (1.0 / math.sqrt(2.0 * math.pi))
    return normal_cdf + values * density


def zt_table(mode_z, mode_t, z_length, t_length):
    positions = jnp.arange(z_length * t_length, dtype=jnp.int32)
    z_index = positions // t_length
    t_index = positions % t_length
    z_phase = z_index[:, None] * mode_z[None, :] % z_length
    t_phase = t_index[:, None] * mode_t[None, :] % t_length
    phases = (z_phase[:, :, None] * t_length + t_phase[:, None, :] * z_length) % (
        z_length * t_length
    )
    angles = phases.reshape(z_length * t_length, -1).astype(jnp.float32) * (
        2.0 * math.pi / (z_length * t_length)
    )
    return jnp.concatenate([jnp.cos(angles), -jnp.sin(angles)], axis=1)


def line_table(mode_list, length):
    phases = mode_list[:, None] * jnp.arange(length, dtype=jnp.int32)[None, :] % length
    angles = phases.astype(jnp.float32) * (2.0 * math.pi / length)
    return (jnp.cos(angles), jnp.sin(angles))


def rotate(real_part, imag_part, pattern, cosine_table, sine_table, direction):
    real_cos = jnp.einsum(pattern, real_part, cosine_table, precision=HIGH)
    real_sin = jnp.einsum(pattern, real_part, sine_table, precision=HIGH)
    imag_cos = jnp.einsum(pattern, imag_part, cosine_table, precision=HIGH)
    imag_sin = jnp.einsum(pattern, imag_part, sine_table, precision=HIGH)
    return (real_cos + direction * imag_sin, imag_cos - direction * real_sin)


def body(field, grad_out, local_weight, mode_weight, mode_x, mode_y, mode_z, mode_t):
    batch_size, channels, x_local, y_local, cell_count = field.shape
    x_total = x_local * lax.axis_size("sx")
    y_total = y_local * lax.axis_size("sy")
    modes_x = mode_x.shape[0]
    modes_y = mode_y.shape[0]
    zt_count = mode_z.shape[0] * mode_t.shape[0]
    zt_local = zt_count // lax.axis_size("sx")
    kx_local = modes_x // lax.axis_size("sy")
    forward_scale = 1.0 / math.sqrt(x_total * y_total * NZ * NT)
    inverse_scale = 1.0 / math.sqrt(modes_x * modes_y * zt_count)
    spectral_table = zt_table(mode_z, mode_t, NZ, NT)
    cos_x, sin_x = line_table(mode_x, x_total)
    cos_y, sin_y = line_table(mode_y, y_total)
    y_start = lax.axis_index("sy") * y_local
    own_cos_y = lax.dynamic_slice_in_dim(cos_y, y_start, y_local, 1)
    own_sin_y = lax.dynamic_slice_in_dim(sin_y, y_start, y_local, 1)

    def along_x(local_block):
        real_part, imag_part = rotate(
            local_block[:, 0], local_block[:, 1], "bjxn,kx->bjkn", cos_x, sin_x, 1.0
        )
        return jnp.stack([real_part, imag_part], axis=1)

    def back_zt(local_block):
        flattened = local_block.reshape(
            local_block.shape[0], 2 * zt_count, x_local, channels, y_local
        )
        return jnp.einsum("bkxcy,sk->bcxys", flattened, spectral_table, precision=HIGH)

    def add_piece(portion):
        kx_count = portion.shape[4]
        real_part, imag_part = rotate(
            portion[:, 0], portion[:, 1], "bcjkl,ly->bjkcy", own_cos_y, own_sin_y, -1.0
        )
        real_part = real_part.reshape(batch_size, zt_local, kx_count, channels * y_local)
        imag_part = imag_part.reshape(batch_size, zt_local, kx_count, channels * y_local)
        real_x, imag_x = rotate(real_part, imag_part, "bjkn,kx->bjxn", cos_x, sin_x, -1.0)
        return jnp.stack([real_x, imag_x], axis=1)

    def transform(values, factor):
        spectra = jnp.einsum("bcxys,sk->bkxcy", values, spectral_table, precision=HIGH)
        spectra = spectra.reshape(batch_size, 2, zt_count, x_local, channels * y_local)
        mixed_x = along_x(lax.all_to_all(spectra, "sx", split_axis=2, concat_axis=3, tiled=True))
        mixed_x = mixed_x.reshape(batch_size, 2, zt_local, modes_x, channels, y_local)
        real_part, imag_part = rotate(
            mixed_x[:, 0], mixed_x[:, 1], "bjkcy,ly->bcjkl", own_cos_y, own_sin_y, 1.0
        )
        partial_sums = jnp.stack([real_part, imag_part], axis=1)
        owned = lax.psum_scatter(partial_sums, "sy", scatter_dimension=4, tiled=True)
        return owned.reshape(batch_size, 2, channels, -1) * factor

    def untransform(spectrum, factor):
        shaped = spectrum.reshape(batch_size, 2, channels, zt_local, kx_local, modes_y)
        field_x = add_piece(lax.all_gather(shaped, "sy", axis=4, tiled=True))
        field_x = field_x * factor
        return back_zt(lax.all_to_all(field_x, "sx", split_axis=3, concat_axis=2, tiled=True))

    spectrum = transform(field, forward_scale)
    x_real, x_imag = (spectrum[:, 0], spectrum[:, 1])
    weight_real, weight_imag = (mode_weight[0], mode_weight[1])
    y_real = jnp.einsum("bcm,com->bom", x_real, weight_real, precision=HIGH) - jnp.einsum(
        "bcm,com->bom", x_imag, weight_imag, precision=HIGH
    )
    y_imag = jnp.einsum("bcm,com->bom", x_imag, weight_real, precision=HIGH) + jnp.einsum(
        "bcm,com->bom", x_real, weight_imag, precision=HIGH
    )
    spectral = untransform(jnp.stack([y_real, y_imag], axis=1), inverse_scale)
    local_term = jnp.einsum("bcxys,co->boxys", field, local_weight, precision=HIGH)
    hidden = spectral + local_term
    upstream = grad_out * gelu_slope(hidden)
    grad_mixed = transform(upstream, inverse_scale)
    dy_real, dy_imag = (grad_mixed[:, 0], grad_mixed[:, 1])
    dx_real = jnp.einsum("bom,com->bcm", dy_real, weight_real, precision=HIGH) + jnp.einsum(
        "bom,com->bcm", dy_imag, weight_imag, precision=HIGH
    )
    dx_imag = jnp.einsum("bom,com->bcm", dy_imag, weight_real, precision=HIGH) - jnp.einsum(
        "bom,com->bcm", dy_real, weight_imag, precision=HIGH
    )
    gw_real = jnp.einsum("bcm,bom->com", x_real, dy_real, precision=HIGH) + jnp.einsum(
        "bcm,bom->com", x_imag, dy_imag, precision=HIGH
    )
    gw_imag = jnp.einsum("bcm,bom->com", x_real, dy_imag, precision=HIGH) - jnp.einsum(
        "bcm,bom->com", x_imag, dy_real, precision=HIGH
    )
    grad_input = untransform(jnp.stack([dx_real, dx_imag], axis=1), forward_scale) + jnp.einsum(
        "boxys,co->bcxys", upstream, local_weight, precision=HIGH
    )
    return (grad_input, jnp.stack([gw_real, gw_imag]))


def solution(mesh):
    placed = (
        P(None, None, "sx", "sy", None),
        P(None, None, "sx", "sy", None),
        P(),
        P(None, None, None, ("sx", "sy")),
        P(),
        P(),
        P(),
        P(),
    )
    return jax.shard_map(
        body,
        mesh=mesh,
        in_specs=placed,
        out_specs=(P(None, None, "sx", "sy", None), P(None, None, None, ("sx", "sy"))),
        check_vma=False,
    )
```

profile of v0, /device:TPU:1, one launch (start us, length us, event | category | flops | bytes accessed | tf_op | source)
XLA Modules:
  0.0 670.9 jit_solution(14436572177904717923)
XLA Ops:
  9.0 2.1 fusion.85
  11.1 7.9 %fusion.11 = f32[2,256,4,16,8]{1,3,4,2,0:T(8,128)S(1)} fusion(f32[2,16,4,8,1024]{4,3,2,1,0:T(8,128)} %param.8, f32[1024,128]{1,0:T(8,128)S(1)} %get-tuple-element.15, f32[1024,128]{1,0:T(8,128)S(1)} %get-tuple-element.14), kind=kOutput, calls=%fused_computation.14 | convolution fusion | flops 3221487616 | bytes 6291456 | tf_op jit(solution)/shard_map/bcxys,sk->bkxcy/dot_general | solution.py:91
  21.6 11.1 %all-to-all-start = ((f32[2,2,128,4,128]{4,3,1,0,2:T(4,128)}), f32[2,2,128,4,128]{4,3,1,0,2:T(4,128)S(1)}, u32[]{:S(2)}, u32[]{:S(2)}) async-start(f32[2,2,128,4,128]{4,3,1,0,2:T(4,128)} %copy.152), calls=%async_computation | async-start | bytes 2097152 | tf_op jit(solution)/shard_map/all_to_all | solution.py:93
  33.2 25.9 %all-to-all-done = f32[2,2,128,4,128]{4,3,1,0,2:T(4,128)S(1)} async-done(((f32[2,2,128,4,128]{4,3,1,0,2:T(4,128)}), f32[2,2,128,4,128]{4,3,1,0,2:T(4,128)S(1)}, u32[]{:S(2)}, u32[]{:S(2)}) %all-to-all-start) | async-done | bytes 1048608 | tf_op jit(solution)/shard_map/all_to_all | solution.py:93
  71.1 108.8 %all-reduce.5.cloned.1.call-done = f32[2,2,16,4,16,16]{2,5,4,3,0,1:T(8,128)} async-done(((f32[2,2,16,4,16,16]{2,5,4,3,0,1:T(8,128)}), f32[2,2,16,4,16,16]{2,5,4,3,0,1:T(8,128)}) %all-reduce.5.cloned.1.call-update) | async-done | bytes 262160
  185.4 44.4 %all_gather.6 = f32[2,2,16,4,16,16]{5,2,3,1,0,4:T(8,128)S(1)} all-gather(f32[2,2,16,4,2,16]{5,2,3,1,0,4:T(8,128)S(1)} %pad_maximum_fusion.2), channel_id=1, replica_groups=mesh['sx'=32,'sy'=8] {'sy'}, dimensions={4}, use_global_device_ids=true | all-gather | bytes 294912 | tf_op jit(solution)/shard_map/all_gather | solution.py:104
  230.0 7.4 %fusion.52 = f32[8,2,16,4,16]{4,0,3,2,1:T(8,128)S(1)} fusion(f32[2,1,16,4,16,16]{5,2,3,1,0,4:T(8,128)S(1)} %get-tuple-element.12, f32[16,64]{0,1:T(8,128)S(1)} %fusion.93, s32[]{:T(128)S(6)} %select_n.70), kind=kOutput, calls=%fused_computation.85 | convolution fusion | flops 3145728 | bytes 1118212 | tf_op jit(solution)/shard_map/bcjkl,ly->bjkcy/dot_general | solution.py:43
  237.4 7.4 %fusion.53 = f32[8,2,16,4,16]{4,0,3,2,1:T(8,128)S(1)} fusion(f32[2,1,16,4,16,16]{5,2,3,1,0,4:T(8,128)S(1)} %get-tuple-element.13, f32[16,64]{0,1:T(8,128)S(1)} %fusion.93, s32[]{:T(128)S(6)} %select_n.70), kind=kOutput, calls=%fused_computation.86 | convolution fusion | flops 3145728 | bytes 1118212 | tf_op jit(solution)/shard_map/bcjkl,ly->bjkcy/dot_general | solution.py:45
  244.8 7.4 %fusion.27 = f32[2,4,16,16,8]{2,4,1,3,0:T(8,128)S(1)} fusion(f32[8,2,16,4,16]{4,0,3,2,1:T(8,128)S(1)} %fusion.52, f32[2,1,16,4,16,16]{5,2,3,1,0,4:T(8,128)S(1)} %get-tuple-element.13, f32[16,64]{0,1:T(8,128)S(1)} %fusion.93, s32[]{:T(128)S(6)} %select_n.70), kind=kOutput, calls=%fused_computation.39 | convolution fusion | flops 3178496 | bytes 1642500 | tf_op jit(solution)/shard_map/bcjkl,ly->bjkcy/dot_general | solution.py:46
  252.3 7.8 %fusion.25 = f32[2,4,16,16,8]{2,4,1,3,0:T(8,128)S(1)} fusion(f32[8,2,16,4,16]{4,0,3,2,1:T(8,128)S(1)} %fusion.53, f32[2,1,16,4,16,16]{5,2,3,1,0,4:T(8,128)S(1)} %get-tuple-element.12, f32[16,64]{0,1:T(8,128)S(1)} %fusion.93, s32[]{:T(128)S(6)} %select_n.70), kind=kOutput, calls=%fused_computation.36 | convolution fusion | flops 3178496 | bytes 1642500 | tf_op jit(solution)/shard_map/bcjkl,ly->bjkcy/dot_general | solution.py:44
  264.0 35.9 %all_to_all.66 = f32[2,2,4,128,128]{4,2,0,1,3:T(4,128)S(1)} all-to-all(f32[2,2,4,128,128]{4,2,0,1,3:T(4,128)S(1)} %copy.174), channel_id=1, replica_groups=mesh['sx'=32,'sy'=8] {'sx'}, dimensions={3} | all-to-all | bytes 2097152 | tf_op jit(solution)/shard_map/all_to_all | solution.py:106
  300.3 11.0 %reshape.166 = f32[2,256,4,16,8]{4,3,2,1,0:T(8,128)} reshape(f32[2,2,32,4,4,128]{5,4,3,2,1,0:T(4,128)S(1)} %bitcast.355) | data formatting | bytes 2097152 | tf_op jit(solution)/shard_map/reshape | solution.py:75
  311.4 12.0 %copy.176 = f32[2,256,4,16,8]{1,3,4,2,0:T(8,128)S(1)} copy(f32[2,256,4,16,8]{4,3,2,1,0:T(8,128)} %reshape.166) | data formatting | bytes 2097152 | tf_op jit(solution)/shard_map/reshape | solution.py:75
  323.4 4.9 fusion.84
  328.3 13.0 %fusion.4 = f32[2,16,4,8,1024]{4,1,3,2,0:T(8,128)S(1)} fusion(f32[2,16,4,8,1024]{4,3,2,1,0:T(8,128)} %param.9, f32[1024,2,4,16,8]{0,3,4,2,1:T(8,128)S(1)} %fusion.84, f32[2,16,4,8,1024]{4,3,2,1,0:T(8,128)S(1)} %copy-done.9, f32[16,16]{1,0:T(8,128)S(1)} %copy-done), kind=kOutput, calls=%fused_computation.5 | convolution fusion | flops 211812352 | bytes 16778240 | tf_op jit(solution)/shard_map/bcxys,co->boxys/dot_general | solution.py:118
  341.3 3.4 convolution_bitcast_fusion
  348.5 32.2 %all_to_all.67 = f32[2,2,128,4,128]{4,3,1,0,2:T(4,128)S(1)} all-to-all(f32[2,2,128,4,128]{4,3,1,0,2:T(4,128)S(1)} %copy.181), channel_id=1, replica_groups=mesh['sx'=32,'sy'=8] {'sx'}, dimensions={2} | all-to-all | bytes 2097152 | tf_op jit(solution)/shard_map/all_to_all | solution.py:93
  392.2 109.3 %all-reduce.7.cloned.1.call-done = f32[2,2,16,4,16,16]{2,5,4,3,0,1:T(8,128)} async-done(((f32[2,2,16,4,16,16]{2,5,4,3,0,1:T(8,128)}), f32[2,2,16,4,16,16]{2,5,4,3,0,1:T(8,128)}) %all-reduce.7.cloned.1.call-update) | async-done | bytes 262160
  508.0 2.2 convolution_subtract_fusion.3
  510.4 44.2 %all_gather.7 = f32[2,2,16,4,16,16]{5,2,3,1,0,4:T(8,128)S(1)} all-gather(f32[2,2,16,4,2,16]{5,2,3,1,0,4:T(8,128)S(1)} %pad_maximum_fusion.3), channel_id=1, replica_groups=mesh['sx'=32,'sy'=8] {'sy'}, dimensions={4}, use_global_device_ids=true | all-gather | bytes 294912 | tf_op jit(solution)/shard_map/all_gather | solution.py:104
  554.8 7.4 %fusion.54 = f32[8,2,16,4,16]{4,0,3,2,1:T(8,128)S(1)} fusion(f32[2,1,16,4,16,16]{5,2,3,1,0,4:T(8,128)S(1)} %get-tuple-element.10, f32[16,64]{0,1:T(8,128)S(1)} %fusion.93, s32[]{:T(128)S(6)} %select_n.70), kind=kOutput, calls=%fused_computation.87 | convolution fusion | flops 3145728 | bytes 1118212 | tf_op jit(solution)/shard_map/bcjkl,ly->bjkcy/dot_general | solution.py:43
  562.3 7.4 %fusion.55 = f32[8,2,16,4,16]{4,0,3,2,1:T(8,128)S(1)} fusion(f32[2,1,16,4,16,16]{5,2,3,1,0,4:T(8,128)S(1)} %get-tuple-element.11, f32[16,64]{0,1:T(8,128)S(1)} %fusion.93, s32[]{:T(128)S(6)} %select_n.70), kind=kOutput, calls=%fused_computation.88 | convolution fusion | flops 3145728 | bytes 1118212 | tf_op jit(solution)/shard_map/bcjkl,ly->bjkcy/dot_general | solution.py:45
  569.7 7.4 %fusion.23 = f32[2,4,16,16,8]{2,4,1,3,0:T(8,128)S(1)} fusion(f32[8,2,16,4,16]{4,0,3,2,1:T(8,128)S(1)} %fusion.54, f32[2,1,16,4,16,16]{5,2,3,1,0,4:T(8,128)S(1)} %get-tuple-element.11, f32[16,64]{0,1:T(8,128)S(1)} %fusion.93, s32[]{:T(128)S(6)} %select_n.70), kind=kOutput, calls=%fused_computation.33 | convolution fusion | flops 3178496 | bytes 1642500 | tf_op jit(solution)/shard_map/bcjkl,ly->bjkcy/dot_general | solution.py:46
  577.2 7.6 %fusion.21 = f32[2,4,16,16,8]{2,4,1,3,0:T(8,128)S(1)} fusion(f32[8,2,16,4,16]{4,0,3,2,1:T(8,128)S(1)} %fusion.55, f32[2,1,16,4,16,16]{5,2,3,1,0,4:T(8,128)S(1)} %get-tuple-element.10, f32[16,64]{0,1:T(8,128)S(1)} %fusion.93, s32[]{:T(128)S(6)} %select_n.70), kind=kOutput, calls=%fused_computation.30 | convolution fusion | flops 3178496 | bytes 1642500 | tf_op jit(solution)/shard_map/bcjkl,ly->bjkcy/dot_general | solution.py:44
  589.6 9.7 %all-to-all-start.3 = ((f32[2,2,4,128,128]{4,2,0,1,3:T(4,128)}), f32[2,2,4,128,128]{4,2,0,1,3:T(4,128)S(1)}, u32[]{:S(2)}, u32[]{:S(2)}) async-start(f32[2,2,4,128,128]{4,2,0,1,3:T(4,128)} %copy.201), calls=%async_computation.3 | async-start | bytes 2097152 | tf_op jit(solution)/shard_map/all_to_all | solution.py:106
  601.1 1.8 fusion.14
  608.3 17.4 %all-to-all-done.3 = f32[2,2,4,128,128]{4,2,0,1,3:T(4,128)S(1)} async-done(((f32[2,2,4,128,128]{4,2,0,1,3:T(4,128)}), f32[2,2,4,128,128]{4,2,0,1,3:T(4,128)S(1)}, u32[]{:S(2)}, u32[]{:S(2)}) %all-to-all-start.3) | async-done | bytes 1048608 | tf_op jit(solution)/shard_map/all_to_all | solution.py:106
  626.2 11.0 %reshape.170 = f32[2,256,4,16,8]{4,3,2,1,0:T(8,128)} reshape(f32[2,2,32,4,4,128]{5,4,3,2,1,0:T(4,128)S(1)} %bitcast.356) | data formatting | bytes 2097152 | tf_op jit(solution)/shard_map/reshape | solution.py:75
  637.2 12.3 %copy.203 = f32[2,256,4,16,8]{1,3,4,2,0:T(8,128)S(1)} copy(f32[2,256,4,16,8]{4,3,2,1,0:T(8,128)} %reshape.170) | data formatting | bytes 2097152 | tf_op jit(solution)/shard_map/reshape | solution.py:75
  649.6 3.8 fusion.83
  653.4 6.0 bitcast_add_fusion
  659.4 4.4 copy.206
  (118 shorter events, 60.3 us)
Async XLA Ops:
  7.2 321.1 %copy-start = (f32[16,16]{1,0:T(8,128)S(1)}, f32[16,16]{1,0:T(8,128)}, u32[]{:S(2)}) copy-start(f32[16,16]{1,0:T(8,128)} %param.10) | copy-start | bytes 3076
  11.1 8.0 %copy-start.3 = (f32[1024,128]{1,0:T(8,128)}, f32[1024,128]{1,0:T(8,128)S(1)}, u32[]{:S(2)}) copy-start(f32[1024,128]{1,0:T(8,128)S(1)} %get-tuple-element.14) | copy-start | bytes 1572868
  11.1 8.0 %copy-start.6 = (f32[1024,128]{1,0:T(8,128)}, f32[1024,128]{1,0:T(8,128)S(1)}, u32[]{:S(2)}) copy-start(f32[1024,128]{1,0:T(8,128)S(1)} %get-tuple-element.15) | copy-start | bytes 1572868
  19.1 14.1 %copy-start.12 = (s32[16]{0:T(128)S(1)}, s32[16]{0:T(128)}, u32[]{:S(2)}) copy-start(s32[16]{0:T(128)} %param.13) | copy-start | bytes 196
  20.2 39.9 %copy-start.11 = (s32[16]{0:T(128)S(1)}, s32[16]{0:T(128)}, u32[]{:S(2)}) copy-start(s32[16]{0:T(128)} %param.12) | copy-start | bytes 196
  21.6 37.5 %all-to-all-start = ((f32[2,2,128,4,128]{4,3,1,0,2:T(4,128)}), f32[2,2,128,4,128]{4,3,1,0,2:T(4,128)S(1)}, u32[]{:S(2)}, u32[]{:S(2)}) async-start(f32[2,2,128,4,128]{4,3,1,0,2:T(4,128)} %copy.152), calls=%async_computation | async-start | bytes 2097152 | tf_op jit(solution)/shard_map/all_to_all | solution.py:93
  32.6 147.2 %all-reduce.5.cloned.1.call-start = ((), (), s32[]{:S(2)}) async-start(), calls=%async_computation.4 | async-start | bytes 4194304
  66.1 2.7 copy-start.10
  67.2 2.6 copy-start.13
  68.7 432.8 %all-reduce.7.cloned.1.call-start = ((), (), s32[]{:S(2)}) async-start(), calls=%async_computation.5 | async-start | bytes 4194304
  323.4 4.9 copy-start.9
  328.3 13.0 %copy-start.4 = (f32[1024,128]{1,0:T(8,128)S(1)}, f32[1024,128]{1,0:T(8,128)}, u32[]{:S(2)}) copy-start(f32[1024,128]{1,0:T(8,128)} %copy-done.3) | copy-start | bytes 1572868
  328.3 13.0 %copy-start.7 = (f32[1024,128]{1,0:T(8,128)S(1)}, f32[1024,128]{1,0:T(8,128)}, u32[]{:S(2)}) copy-start(f32[1024,128]{1,0:T(8,128)} %copy-done.6) | copy-start | bytes 1572868
  341.3 3.5 copy-start.1
  589.6 36.1 %all-to-all-start.3 = ((f32[2,2,4,128,128]{4,2,0,1,3:T(4,128)}), f32[2,2,4,128,128]{4,2,0,1,3:T(4,128)S(1)}, u32[]{:S(2)}, u32[]{:S(2)}) async-start(f32[2,2,4,128,128]{4,2,0,1,3:T(4,128)} %copy.201), calls=%async_computation.3 | async-start | bytes 2097152 | tf_op jit(solution)/shard_map/all_to_all | solution.py:106
  637.2 12.4 %copy-start.5 = (f32[1024,128]{1,0:T(8,128)S(1)}, f32[1024,128]{1,0:T(8,128)}, u32[]{:S(2)}) copy-start(f32[1024,128]{1,0:T(8,128)} %copy-done.3) | copy-start | bytes 1572868
  637.2 12.4 %copy-start.8 = (f32[1024,128]{1,0:T(8,128)S(1)}, f32[1024,128]{1,0:T(8,128)}, u32[]{:S(2)}) copy-start(f32[1024,128]{1,0:T(8,128)} %copy-done.6) | copy-start | bytes 1572868
  649.6 3.8 copy-start.2
Sparse Core Ops, SparseCore 0:
  68.9 110.9 all-reduce.4
  392.3 109.1 all-reduce.6
where the time goes:
time: 678 us; the launch traced here: 671 us
  waiting for transfers between devices  261 us (38%)
  blocking collectives  157 us (23%)
  matrix products  136 us (20%)
  local copies, waits for them, and re-layouts  69.9 us (10%)
  starting transfers between devices  21.3 us (3%)
  between operations  15.7 us (2%)
  other arithmetic  9.55 us (1%)
    unnamed x4, waiting for transfers between devices  218 us
    all_gather x2, blocking collectives, untransform(): field_x = add_piece(lax.all_gather(shaped, 'sy', axis=4, tiled=True))  88.5 us
    reshape x4, local copies, waits for them, and re-layouts, back_zt(): local_block.reshape(local_block.shape[0], 2 * zt_count, x_local, channels...  46.4 us
    all_to_all x1, blocking collectives, untransform(): lax.all_to_all(field_x, 'sx', split_axis=3, concat_axis=2, tiled=True)  35.9 us
    all_to_all x1, blocking collectives, transform(): lax.all_to_all(spectra, 'sx', split_axis=2, concat_axis=3, tiled=True)  32.2 us
    all_to_all x1, waiting for transfers between devices, transform(): lax.all_to_all(spectra, 'sx', split_axis=2, concat_axis=3, tiled=True)  25.9 us
    dot_general x8, matrix products, rotate(): real_sin = jnp.einsum(pattern, real_part, sine_table, precision=HIGH)  20 us
    dot_general x8, matrix products, rotate(): imag_sin = jnp.einsum(pattern, imag_part, sine_table, precision=HIGH)  19.5 us
  transfers between devices with their start and end apart: 4, of which 4 were waited for; matrix products, arithmetic and copies ran while one was open for 2% of the time, Pallas kernels for 0%

commit v1 on v0

v1 whole, which is shorter than its diff:
```python
import functools
import math

import jax
import jax.numpy as jnp
from jax import lax
from jax.experimental import pallas as pl
from jax.experimental.pallas import tpu as pltpu
from jax.sharding import PartitionSpec as P

MESH = pl.DeviceIdType.MESH
F32 = jnp.float32
BF16 = jnp.bfloat16
NSX = 32
NSY = 8
FORWARD = 1.0 / math.sqrt(128 * 64 * 1024)
INVERSE = 1.0 / math.sqrt(32768)
ROOT_HALF = 1.0 / math.sqrt(2.0)
DENSITY = 1.0 / math.sqrt(2.0 * math.pi)


def iota(shape, dim):
    return lax.broadcasted_iota(jnp.int32, shape, dim)


def split(values):
    high = values.astype(BF16)
    return high, (values - high.astype(F32)).astype(BF16)


def dot(a, b, contract=(1, 0)):
    return lax.dot_general(
        a, b, (((contract[0],), (contract[1],)), ((), ())), preferred_element_type=F32
    )


def dot3(a_high, a_low, b_high, b_low, contract=(1, 0)):
    total = dot(a_high, b_high, contract)
    total += dot(a_high, b_low, contract)
    return total + dot(a_low, b_high, contract)


def mul3(a, b):
    return dot3(*split(a), *split(b))


def turn(phase, length):
    angle = phase.astype(F32) * (2.0 * math.pi / length)
    return jnp.cos(angle), jnp.sin(angle)


def pick(index, mode_ref, count):
    total = jnp.zeros(index.shape, jnp.int32)
    for k in range(count):
        total = jnp.where(index == k, mode_ref[k], total)
    return total


def tables_kernel(
    mx_ref, my_ref, mz_ref, mt_ref, lw_ref, th_ref, tl_ref, tx_ref, txi_ref, ty_ref, tyi_ref, kf_ref, kb_ref
):
    pair = iota((64, 128), 1)
    cz, sz = turn((iota((64, 128), 0) * pick(pair // 8, mz_ref, 16)) & 63, 64)
    pair = iota((16, 128), 1)
    ct, st = turn((iota((16, 128), 0) * pick(pair % 8, mt_ref, 8)) & 15, 16)
    cz, sz = cz[:, None, :], sz[:, None, :]
    real = (cz * ct - sz * st).reshape(1024, 128)
    imag = (-(sz * ct) - cz * st).reshape(1024, 128)
    high, low = split(real)
    th_ref[:, :128] = high
    tl_ref[:, :128] = low
    high, low = split(imag)
    th_ref[:, 128:] = high
    tl_ref[:, 128:] = low
    row, col = iota((64, 256), 0), iota((64, 256), 1)
    c, s = turn(((col // 2) * pick((row // 8) * 2 + (row // 2) % 2, mx_ref, 16)) & 127, 128)
    ro, ri = row % 2, col % 2
    value = jnp.where(ro == ri, c, jnp.where(ro == 0, s, -s))
    tx_ref[...] = jnp.where(row % 8 < 4, value, 0.0)
    row, col = iota((256, 64), 0), iota((256, 64), 1)
    c, s = turn(((row // 2) * pick((col // 8) * 2 + (col // 2) % 2, mx_ref, 16)) & 127, 128)
    ro, ri = row % 2, col % 2
    value = jnp.where(ro == ri, c, jnp.where(ro == 0, -s, s))
    txi_ref[...] = jnp.where(col % 8 < 4, value, 0.0)
    row, col = iota((128, 256), 0), iota((128, 256), 1)
    c, s = turn(((col % 64) * pick(row % 16, my_ref, 16)) & 63, 64)
    same = (row // 64 == col // 128) & ((row // 16) % 2 == (col // 64) % 2)
    ty_ref[...] = jnp.where(same, jnp.where((row // 32) % 2 == 0, c, s), 0.0)
    row, col = iota((512, 128), 0), iota((512, 128), 1)
    y = ((row // 32) % 8) * 8 + row % 8
    c, s = turn((y * pick(col % 16, my_ref, 16)) & 63, 64)
    ro, ri = row // 256, (col // 32) % 2
    same = ((row // 8) % 2 == col // 64) & ((row // 16) % 2 == (col // 16) % 2)
    value = jnp.where(ro == ri, c, jnp.where(ro == 0, -s, s))
    tyi_ref[...] = jnp.where(same, value, 0.0)
    row, col = iota((256, 16), 0), iota((256, 16), 1)
    spread = jnp.where(row // 16 == col, 1.0, 0.0)
    weight = lw_ref[...]
    wide = lax.dot_general(
        spread, weight, (((1,), (0,)), ((), ())), precision=lax.Precision.HIGHEST, preferred_element_type=F32
    )
    wide = lax.dot_general(
        wide, spread, (((1,), (1,)), ((), ())), precision=lax.Precision.HIGHEST, preferred_element_type=F32
    )
    row, col = iota((256, 256), 0), iota((256, 256), 1)
    wide = jnp.where(row % 16 == col % 16, wide, 0.0)
    kb_ref[...] = wide
    kf_ref[...] = wide.T


def make_tables(mode_x, mode_y, mode_z, mode_t, local_weight):
    shape = jax.ShapeDtypeStruct
    smem = pl.BlockSpec(memory_space=pltpu.SMEM)
    vmem = pl.BlockSpec(memory_space=pltpu.VMEM)
    return pl.pallas_call(
        tables_kernel,
        out_shape=(
            shape((1024, 256), BF16),
            shape((1024, 256), BF16),
            shape((64, 256), F32),
            shape((256, 64), F32),
            shape((128, 256), F32),
            shape((512, 128), F32),
            shape((256, 256), F32),
            shape((256, 256), F32),
        ),
        in_specs=[smem, smem, smem, smem, vmem],
        out_specs=[vmem] * 8,
        compiler_params=pltpu.CompilerParams(vmem_limit_bytes=24 << 20),
        name="tables",
    )(mode_x, mode_y, mode_z, mode_t, local_weight)


def swap_lanes(first, second, width):
    low = (iota(first.shape, 1) // width) % 2 == 0
    return (
        jnp.where(low, first, pltpu.roll(second, width, 1)),
        jnp.where(low, pltpu.roll(first, 128 - width, 1), second),
    )


def swap_four(parts):
    a, b, c, d = parts
    a, c = swap_lanes(a, c, 64)
    b, d = swap_lanes(b, d, 64)
    a, b = swap_lanes(a, b, 32)
    c, d = swap_lanes(c, d, 32)
    return a, b, c, d


def gelu_slope(values):
    normal_cdf = 0.5 * (1.0 + lax.erf(values * ROOT_HALF))
    return normal_cdf + values * (jnp.exp(-0.5 * values * values) * DENSITY)


def chain_kernel(
    field_ref, gout_ref, w_ref, th_ref, tl_ref, tx_ref, txi_ref, ty_ref, tyi_ref, kf_ref,
    uh_out, ul_out, last_out, gm_ref,
    field, gout, fh, fl, uh, ul, sa, ra, sb, rb, sc, rc, turned, spectra, slopes, mixed,
    load_sem, store_sem, sa_send, sa_recv, sa_own, sb_send, sb_recv, sb_own, sc_send, sc_recv, sc_own,
):
    sx, sy = lax.axis_index("sx"), lax.axis_index("sy")

    def load(b, which):
        source, target = ((field_ref, field), (gout_ref, gout))[which]
        return pltpu.make_async_copy(source.at[b], target.at[b], load_sem.at[which, b])

    for which in range(2):
        for b in range(2):
            load(b, which).start()

    barrier = pltpu.get_barrier_semaphore()

    def greet(axis, me, n):
        def one(d, carry):
            pl.semaphore_signal(
                barrier, inc=1, device_id={axis: lax.rem(me + d, n)}, device_id_type=MESH
            )
            return carry

        lax.fori_loop(1, n, one, 0)

    greet("sy", sy, NSY)
    greet("sx", sx, NSX)

    def exchange(axis, me, n, source, target, send, recv, own):
        def one(d, carry):
            to = lax.rem(me + d, n)
            pltpu.make_async_remote_copy(
                src_ref=source(to),
                dst_ref=target(me),
                send_sem=send,
                recv_sem=recv,
                device_id={axis: to},
                device_id_type=MESH,
            ).start()
            return carry

        lax.fori_loop(1, n, one, 0)
        pltpu.make_async_copy(source(me), target(me), own).start()

    def drain(whole, one, sem, own=None):
        pltpu.make_async_copy(whole, whole, sem).wait()
        if own is not None:
            pltpu.make_async_copy(one, one, own).wait()

    def start_a(k, b):
        target = (lambda d: ra.at[k, b, d]) if k < 3 else (lambda d: last_out.at[b, d])
        exchange(
            "sy", sy, NSY, lambda d: sa.at[k, b, d], target, sa_send.at[k, b], sa_recv.at[k, b], sa_own.at[k, b]
        )

    def wait_a(k, b):
        whole = ra.at[k, b] if k < 3 else last_out.at[b]
        drain(whole.at[pl.ds(0, NSY - 1)], whole.at[0], sa_recv.at[k, b], sa_own.at[k, b])

    def start_b(k, b):
        rows = lambda d: pl.ds(pl.multiple_of(d * 8, 8), 8)
        exchange(
            "sx", sx, NSX, lambda d: sb.at[k, b, rows(d)], lambda d: rb.at[k, b, rows(d)],
            sb_send.at[k, b], sb_recv.at[k, b], sb_own.at[k, b],
        )

    def wait_b(k, b):
        whole = rb.at[k, b]
        drain(whole.at[pl.ds(0, (NSX - 1) * 8)], whole.at[pl.ds(0, 8)], sb_recv.at[k, b], sb_own.at[k, b])

    def start_c(k, b):
        rows = lambda d: pl.ds(pl.multiple_of(d * 8, 8), 8)
        exchange(
            "sy", sy, NSY, lambda d: sc.at[k, b, rows(d)], lambda d: rc.at[k, b, rows(d)],
            sc_send.at[k, b], sc_recv.at[k, b], sc_own.at[k, b],
        )

    def wait_c(k, b):
        whole = rc.at[k, b]
        drain(whole.at[pl.ds(0, (NSY - 1) * 8)], whole.at[pl.ds(0, 8)], sc_recv.at[k, b], sc_own.at[k, b])

    def zt_forward(k, b, high_ref, low_ref, source=None):
        def block(m, carry):
            rows = pl.ds(m * 8, 8)
            if source is None:
                high = high_ref[b, rows].reshape(256, 1024)
                low = low_ref[b, rows].reshape(256, 1024)
            else:
                high, low = split(source[b, rows].reshape(256, 1024))
                high_ref[b, rows] = high.reshape(8, 32, 1024)
                low_ref[b, rows] = low.reshape(8, 32, 1024)
            out = dot3(high, low, th_ref[...], tl_ref[...])
            sa[k, b, pl.ds(m * 4, 4)] = out.reshape(4, 64, 256)
            return carry

        lax.fori_loop(0, 2, block, 0)

    def y_forward(ka, kb, b):
        for i in range(2):
            parts = [
                ra[ka, b, :, c * 32 + (i * 2 + x) * 8 : c * 32 + (i * 2 + x) * 8 + 8, :].reshape(64, 256)
                for x in range(2)
                for c in range(2)
            ]
            out = mul3(ty_ref[...], jnp.concatenate(parts, axis=0))
            rows = []
            for x in range(2):
                cos, sin = out[x * 64 : x * 64 + 32], out[x * 64 + 32 : x * 64 + 64]
                rows.append(cos[:, :128] + sin[:, 128:])
                rows.append(cos[:, 128:] - sin[:, :128])
            turned[i] = jnp.concatenate(rows, axis=0).T
            parts = swap_four([turned[i, pl.ds(z, 32, stride=4), :] for z in range(4)])
            for q in range(4):
                sb[kb, b, pl.ds(i * 4 + q, 32, stride=8), :] = parts[q]

    def y_backward(kb, ka, b):
        halves = []
        for i in range(2):
            parts = swap_four([rb[kb, b, pl.ds(i * 4 + q, 32, stride=8), :] for q in range(4)])
            for z in range(4):
                turned[i, pl.ds(z, 32, stride=4), :] = parts[z]
            halves.append(turned[i].T)
        out = mul3(tyi_ref[...], jnp.concatenate(halves, axis=1))
        for part in range(2):
            for i in range(2):
                block = out[part * 256 : part * 256 + 256, i * 128 : i * 128 + 128].reshape(8, 2, 16, 128)
                for o in range(2):
                    sa[ka, b, :, o * 32 + i * 16 : o * 32 + i * 16 + 16, part * 128 : part * 128 + 128] = block[:, o]

    def x_forward(kb, kc, b):
        sc[kc, b] = mul3(tx_ref[...], rb[kb, b])

    def x_backward(kc, kb, b):
        sb[kb, b] = mul3(txi_ref[...], rc[kc, b])

    def gather_modes(kc, b, keep, factor):
        for part in range(2):
            pair = swap_lanes(
                rc[kc, b, pl.ds(part, 8, stride=8), :], rc[kc, b, pl.ds(2 + part, 8, stride=8), :], 16
            )
            for low in range(2):
                keep[b, part, pl.ds(low, 8, stride=2), :] = pair[low] * factor

    def spread_modes(kc, b):
        for part in range(2):
            pair = swap_lanes(
                mixed[part, pl.ds(0, 8, stride=2), :], mixed[part, pl.ds(1, 8, stride=2), :], 16
            )
            for kx in range(2):
                sc[kc, b, pl.ds(kx * 2 + part, 8, stride=8), :] = pair[kx]
        for idle in range(4, 8):
            sc[kc, b, pl.ds(idle, 8, stride=8), :] = jnp.zeros((8, 128), F32)

    def mix(kin, kout, b):
        gather_modes(kin, b, spectra, FORWARD)

        def channel(c, carry):
            real, imag = carry
            wr, wi = w_ref[0, c], w_ref[1, c]
            xr, xi = spectra[b, 0, pl.ds(c, 1), :], spectra[b, 1, pl.ds(c, 1), :]
            return real + (wr * xr - wi * xi), imag + (wr * xi + wi * xr)

        zero = jnp.zeros((16, 128), F32)
        real, imag = lax.fori_loop(0, 16, channel, (zero, zero), unroll=4)
        mixed[0] = real * INVERSE
        mixed[1] = imag * INVERSE
        spread_modes(kout, b)

    def mix_back(kin, kout, b):
        gather_modes(kin, b, slopes, INVERSE)
        dr, di = slopes[b, 0], slopes[b, 1]

        def channel(c, carry):
            wr, wi = w_ref[0, c], w_ref[1, c]
            mixed[0, pl.ds(c, 1), :] = jnp.sum(wr * dr + wi * di, axis=0, keepdims=True) * FORWARD
            mixed[1, pl.ds(c, 1), :] = jnp.sum(wr * di - wi * dr, axis=0, keepdims=True) * FORWARD
            return carry

        lax.fori_loop(0, 16, channel, 0, unroll=4)
        spread_modes(kout, b)

    def weight_grad():
        def channel(c, carry):
            real = imag = jnp.zeros((16, 128), F32)
            for b in range(2):
                xr, xi = spectra[b, 0, pl.ds(c, 1), :], spectra[b, 1, pl.ds(c, 1), :]
                dr, di = slopes[b, 0], slopes[b, 1]
                real = real + (xr * dr + xi * di)
                imag = imag + (xr * di - xi * dr)
            gm_ref[0, c] = real
            gm_ref[1, c] = imag
            return carry

        lax.fori_loop(0, 16, channel, 0)

    def slope_stage(ka, b):
        for g in range(2):
            cells = slice(g * 16, g * 16 + 16)
            parts = [ra[ka, b, :, o * 32 + g * 16 : o * 32 + g * 16 + 16, :] for o in range(2)]
            lh, ll = split(jnp.concatenate(parts, axis=1).reshape(256, 256))
            kh, kl = split(kf_ref[...])

            def columns(n, carry):
                cols = pl.ds(pl.multiple_of(n * 256, 256), 256)
                hidden = dot3(lh, ll, th_ref[cols, :], tl_ref[cols, :], (1, 1))
                hidden += dot3(
                    kh, kl, fh[b, :, cells, cols].reshape(256, 256), fl[b, :, cells, cols].reshape(256, 256)
                )
                upstream = gout[b, :, cells, cols].reshape(256, 256) * gelu_slope(hidden)
                high, low = split(upstream)
                uh[b, :, cells, cols] = high.reshape(16, 16, 256)
                ul[b, :, cells, cols] = low.reshape(16, 16, 256)
                return carry

            lax.fori_loop(0, 4, columns, 0)

    def store(b):
        return (
            pltpu.make_async_copy(uh.at[b], uh_out.at[b], store_sem.at[0, b]),
            pltpu.make_async_copy(ul.at[b], ul_out.at[b], store_sem.at[1, b]),
        )

    for b in range(2):
        load(b, 0).wait()
        zt_forward(0, b, fh, fl, field)
        if b == 0:
            pl.semaphore_wait(barrier, NSX + NSY - 2)
        start_a(0, b)
    for b in range(2):
        wait_a(0, b)
        y_forward(0, 0, b)
        start_b(0, b)
    for b in range(2):
        wait_b(0, b)
        x_forward(0, 0, b)
        start_c(0, b)
    for b in range(2):
        wait_c(0, b)
        mix(0, 1, b)
        start_c(1, b)
    for b in range(2):
        wait_c(1, b)
        x_backward(1, 1, b)
        start_b(1, b)
    for b in range(2):
        wait_b(1, b)
        y_backward(1, 1, b)
        start_a(1, b)
    for b in range(2):
        wait_a(1, b)
        load(b, 1).wait()
        slope_stage(1, b)
        zt_forward(2, b, uh, ul)
        start_a(2, b)
        for copy in store(b):
            copy.start()
    for b in range(2):
        wait_a(2, b)
        y_forward(2, 2, b)
        start_b(2, b)
    for b in range(2):
        wait_b(2, b)
        x_forward(2, 2, b)
        start_c(2, b)
    for b in range(2):
        wait_c(2, b)
        mix_back(2, 3, b)
        start_c(3, b)
    for b in range(2):
        wait_c(3, b)
        x_backward(3, 3, b)
        start_b(3, b)
    weight_grad()
    for b in range(2):
        wait_b(3, b)
        y_backward(3, 3, b)
        start_a(3, b)
    for b in range(2):
        wait_a(3, b)
    for b in range(2):
        for k in range(4):
            drain(sa.at[k, b, pl.ds(0, NSY - 1)], None, sa_send.at[k, b])
            drain(sb.at[k, b, pl.ds(0, (NSX - 1) * 8)], None, sb_send.at[k, b])
            drain(sc.at[k, b, pl.ds(0, (NSY - 1) * 8)], None, sc_send.at[k, b])
        for copy in store(b):
            copy.wait()


def chain(field, gout, weight, th, tl, tx, txi, ty, tyi, kf):
    shape = jax.ShapeDtypeStruct
    any_space = pl.BlockSpec(memory_space=pl.ANY)
    vmem = pl.BlockSpec(memory_space=pltpu.VMEM)
    sems = pltpu.SemaphoreType.DMA
    return pl.pallas_call(
        chain_kernel,
        out_shape=(
            shape((2, 16, 32, 1024), BF16),
            shape((2, 16, 32, 1024), BF16),
            shape((2, 8, 64, 256), F32),
            shape((2, 16, 16, 128), F32),
        ),
        in_specs=[any_space] * 2 + [vmem] * 8,
        out_specs=[any_space, any_space, any_space, vmem],
        scratch_shapes=[
            pltpu.VMEM((2, 16, 32, 1024), F32),
            pltpu.VMEM((2, 16, 32, 1024), F32),
            pltpu.VMEM((2, 16, 32, 1024), BF16),
            pltpu.VMEM((2, 16, 32, 1024), BF16),
            pltpu.VMEM((2, 16, 32, 1024), BF16),
            pltpu.VMEM((2, 16, 32, 1024), BF16),
            pltpu.VMEM((4, 2, 8, 64, 256), F32),
            pltpu.VMEM((3, 2, 8, 64, 256), F32),
            pltpu.VMEM((4, 2, 256, 128), F32),
            pltpu.VMEM((4, 2, 256, 128), F32),
            pltpu.VMEM((4, 2, 64, 128), F32),
            pltpu.VMEM((4, 2, 64, 128), F32),
            pltpu.VMEM((2, 128, 128), F32),
            pltpu.VMEM((2, 2, 16, 128), F32),
            pltpu.VMEM((2, 2, 16, 128), F32),
            pltpu.VMEM((2, 16, 128), F32),
            sems((2, 2)),
            sems((2, 2)),
        ]
        + [sems((4, 2))] * 9,
        compiler_params=pltpu.CompilerParams(
            collective_id=1, has_side_effects=True, vmem_limit_bytes=56 << 20
        ),
        name="chain",
    )(field, gout, weight, th, tl, tx, txi, ty, tyi, kf)


def finish_kernel(spectra_ref, uh_ref, ul_ref, th_ref, tl_ref, kb_ref, out_ref):
    parts = [spectra_ref[0, :, o, :, :] for o in range(2)]
    lh, ll = split(jnp.concatenate(parts, axis=1).reshape(256, 256))
    kh, kl = split(kb_ref[...])

    def columns(n, carry):
        cols = pl.ds(pl.multiple_of(n * 256, 256), 256)
        total = dot3(lh, ll, th_ref[cols, :], tl_ref[cols, :], (1, 1))
        total += dot3(
            kh, kl, uh_ref[0, :, :, cols].reshape(256, 256), ul_ref[0, :, :, cols].reshape(256, 256)
        )
        out_ref[0, :, :, cols] = total.reshape(16, 16, 256)
        return carry

    lax.fori_loop(0, 4, columns, 0)


def finish(spectra, uh, ul, th, tl, kb):
    cells = pl.BlockSpec((1, 16, 16, 1024), lambda b, g: (b, 0, g, 0))
    fixed = lambda *shape: pl.BlockSpec(shape, lambda b, g: (0,) * len(shape))
    return pl.pallas_call(
        finish_kernel,
        grid=(2, 2),
        out_shape=jax.ShapeDtypeStruct((2, 16, 32, 1024), F32),
        in_specs=[
            pl.BlockSpec((1, 8, 2, 16, 256), lambda b, g: (b, 0, 0, g, 0)),
            cells,
            cells,
            fixed(1024, 256),
            fixed(1024, 256),
            fixed(256, 256),
        ],
        out_specs=cells,
        compiler_params=pltpu.CompilerParams(vmem_limit_bytes=32 << 20),
        name="finish",
    )(spectra.reshape(2, 8, 2, 32, 256), uh, ul, th, tl, kb)


def body(field, grad_out, local_weight, mode_weight, mode_x, mode_y, mode_z, mode_t):
    th, tl, tx, txi, ty, tyi, kf, kb = make_tables(mode_x, mode_y, mode_z, mode_t, local_weight)
    uh, ul, spectra, grad_modes = chain(
        field.reshape(2, 16, 32, 1024),
        grad_out.reshape(2, 16, 32, 1024),
        mode_weight,
        th, tl, tx, txi, ty, tyi, kf,
    )
    grad_input = finish(spectra, uh, ul, th, tl, kb)
    return grad_input.reshape(field.shape), grad_modes


def solution(mesh):
    grid = P(None, None, "sx", "sy", None)
    modes = P(None, None, None, ("sx", "sy"))
    return jax.shard_map(
        body,
        mesh=mesh,
        in_specs=(grid, grid, P(), modes, P(), P(), P(), P()),
        out_specs=(grid, modes),
        check_vma=False,
    )
```

time: 678 us -> 138 us (0.20); the launches traced: 671 us -> 138 us
  waiting for transfers between devices: 261 us -> 0 us
  blocking collectives: 157 us -> 0 us
  matrix products: 136 us -> 0 us
  Pallas kernels: 0 us -> 124 us
  local copies, waits for them, and re-layouts: 69.9 us -> 13.4 us
  starting transfers between devices: 21.3 us -> 0 us
  between operations: 15.7 us -> 0.7 us
  other arithmetic: 9.55 us -> 0 us
    unnamed x4 -> x0, waiting for transfers between devices: 218 us -> none
    dot_general x50 -> x0, matrix products: 136 us -> none  [the longest x8 20 us: rotate(): real_sin = jnp.einsum(pattern, real_part, sine_table, precision=HIGH)]
    pallas_call x0 -> x3, Pallas kernels: none -> 124 us  [the longest x1 111 us: chain(): pl.pallas_call(chain_kernel, out_shape=(shape((2, 16, 32, 1024), BF16), s...]
    all_gather x2 -> x0, blocking collectives: 88.5 us -> none  [untransform(): field_x = add_piece(lax.all_gather(shaped, 'sy', axis=4, tiled=True))]
    all_to_all x2 -> x0, blocking collectives: 68.2 us -> none  [the longest x1 35.9 us: untransform(): lax.all_to_all(field_x, 'sx', split_axis=3, concat_axis=2, tiled=True)]
    reshape x8 -> x0, local copies, waits for them, and re-layouts: 51.4 us -> none  [the longest x4 46.4 us: back_zt(): local_block.reshape(local_block.shape[0], 2 * zt_count, x_local, channels...]
    all_to_all x2 -> x0, waiting for transfers between devices: 43.3 us -> none  [the longest x1 25.9 us: transform(): lax.all_to_all(spectra, 'sx', split_axis=2, concat_axis=3, tiled=True)]
    all_to_all x2 -> x0, starting transfers between devices: 20.7 us -> none  [the longest x1 11.1 us: transform(): lax.all_to_all(spectra, 'sx', split_axis=2, concat_axis=3, tiled=True)]
  transfers between devices with their start and end apart: 4 -> 0, of which waited for: 4 -> 0; matrix products, arithmetic and copies ran while one was open for 2% -> 0% of each run, Pallas kernels for 0% -> 0%
where the time goes in v1:
time: 138 us
  Pallas kernels  124 us (90%)
  local copies, waits for them, and re-layouts  13.4 us (10%)
    pallas_call x1, Pallas kernels, chain(): pl.pallas_call(chain_kernel, out_shape=(shape((2, 16, 32, 1024), BF16), s...  111 us
    unnamed x37, local copies, waits for them, and re-layouts  13.4 us
    pallas_call x1, Pallas kernels, finish(): pl.pallas_call(finish_kernel, grid=(2, 2), out_shape=jax.ShapeDtypeStruct...  8.14 us
    pallas_call x1, Pallas kernels, make_tables(): pl.pallas_call(tables_kernel, out_shape=(shape((1024, 256), BF16), shape(...  4.31 us

profile of v1, /device:TPU:1, one launch (start us, length us, event | category | flops | bytes accessed | tf_op | source)
XLA Modules:
  0.0 137.9 jit_solution(120971280237307296)
XLA Ops:
  0.6 0.0 copy-start.12
  0.6 0.7 copy-done.12
  1.3 0.0 copy-start.13
  1.3 0.7 copy-done.13
  2.0 0.0 copy-start.14
  2.0 0.7 copy-done.14
  2.6 0.0 copy-start.15
  2.6 0.7 copy-done.15
  3.3 0.0 copy-start.16
  3.3 0.7 copy-done.16
  4.0 4.3 %tables.1 = (bf16[1024,256]{1,0:T(8,128)(2,1)S(1)}, bf16[1024,256]{1,0:T(8,128)(2,1)S(1)}, f32[64,256]{1,0:T(8,128)S(1)}, f32[256,64]{1,0:T(8,128)S(1)}, f32[128...) custom-call(s32[16]{0:T(128)S(1)} %copy-done.13, ...), custom_call_target="tpu_custom_call" | custom-call | tf_op jit(solution)/shard_map/tables/pallas_call | solution.py:115
  8.3 0.0 copy-start.2
  8.3 0.8 copy-done.2
  9.1 0.0 copy-start.4
  9.1 0.8 copy-done.4
  9.9 0.0 copy-start.7
  9.9 0.7 copy-done.7
  10.6 0.0 copy-start.8
  10.6 0.7 copy-done.8
  11.3 0.7 copy-done.9
  12.0 0.6 copy-done.10
  12.6 0.6 copy-done.11
  13.2 111.4 %chain.1 = (bf16[2,16,32,1024]{3,2,1,0:T(8,128)(2,1)}, bf16[2,16,32,1024]{3,2,1,0:T(8,128)(2,1)}, f32[2,8,64,256]{3,2,1,0:T(8,128)}, f32[2,16,16,128]{3,2,1,0:T(8,128)}) custom-call(f32[2,16,32,1024]{3,2,1,0:T(8,128)} %bitcast.5, f32[2,16,32,1024]{3,2,1,0:T(8,128)} %bitcast.6, f32[2,16,16,128]{3,2,1,0:T(8,128)} %w_ref.1, bf16[1024,256]{1,0:T(8,128)(2,1)} %copy-done.2, ...), custom_call_target="tpu_custom_call" | custom-call | tf_op jit(solution)/shard_map/chain/pallas_call | solution.py:451
  124.6 0.0 copy-done.3
  124.6 0.0 copy-done.5
  124.6 0.0 copy-start
  124.6 1.6 %copy-done = bf16[2,16,32,1024]{3,2,1,0:T(8,128)(2,1)S(1)} copy-done((bf16[2,16,32,1024]{3,2,1,0:T(8,128)(2,1)S(1)}, bf16[2,16,32,1024]{3,2,1,0:T(8,128)(2,1)}, u32[]{:S(2)}) %copy-start) | copy-done | bytes 2097176
  126.2 1.6 %copy-done.1 = bf16[2,16,32,1024]{3,2,1,0:T(8,128)(2,1)S(1)} copy-done((bf16[2,16,32,1024]{3,2,1,0:T(8,128)(2,1)S(1)}, bf16[2,16,32,1024]{3,2,1,0:T(8,128)(2,1)}, u32[]{:S(2)}) %copy-start.1) | copy-done | bytes 2097176
  127.8 1.2 copy-done.6
  129.0 8.1 %finish.1 = f32[2,16,32,1024]{3,2,1,0:T(8,128)} custom-call(f32[2,8,2,32,256]{4,3,2,1,0:T(8,128)S(1)} %bitcast.4, bf16[2,16,32,1024]{3,2,1,0:T(8,128)(2,1)S(1)} %copy-done, bf16[2,16,32,1024]{3,2,1,0:T(8,128)(2,1)S(1)} %copy-done.1, bf16[1024,256]{1,0:T(8,128)(2,1)S(1)} %copy-done.3, bf16[1024,256]{1,0:T(8,128)(2,1)S(1)} %copy-done.5, ...), custom_call_target="tpu_custom_call" | custom-call | tf_op jit(solution)/shard_map/finish/pallas_call | solution.py:509
  137.2 0.0 copy-done.17
  137.2 0.7 copy.11
  (8 shorter events, 0.0 us)
Async XLA Ops:
  0.6 0.7 copy-start.12
  1.3 0.7 copy-start.13
  2.0 0.7 copy-start.14
  2.6 0.7 copy-start.15
  3.3 0.7 copy-start.16
  8.3 0.8 copy-start.2
  9.1 0.8 copy-start.4
  9.9 0.7 copy-start.7
  10.6 0.7 copy-start.8
  11.3 0.7 copy-start.9
  12.0 0.6 copy-start.10
  12.6 0.6 copy-start.11
  13.2 111.4 %copy-start.3 = (bf16[1024,256]{1,0:T(8,128)(2,1)S(1)}, bf16[1024,256]{1,0:T(8,128)(2,1)}, u32[]{:S(2)}) copy-start(bf16[1024,256]{1,0:T(8,128)(2,1)} %copy-done.2) | copy-start | bytes 1572868
  13.2 111.4 %copy-start.5 = (bf16[1024,256]{1,0:T(8,128)(2,1)S(1)}, bf16[1024,256]{1,0:T(8,128)(2,1)}, u32[]{:S(2)}) copy-start(bf16[1024,256]{1,0:T(8,128)(2,1)} %copy-done.4) | copy-start | bytes 1572868
  124.6 1.6 %copy-start = (bf16[2,16,32,1024]{3,2,1,0:T(8,128)(2,1)S(1)}, bf16[2,16,32,1024]{3,2,1,0:T(8,128)(2,1)}, u32[]{:S(2)}) copy-start(bf16[2,16,32,1024]{3,2,1,0:T(8,128)(2,1)} %get-tuple-element.22.uh_ref) | copy-start | bytes 6291460
  126.2 1.6 %copy-start.1 = (bf16[2,16,32,1024]{3,2,1,0:T(8,128)(2,1)S(1)}, bf16[2,16,32,1024]{3,2,1,0:T(8,128)(2,1)}, u32[]{:S(2)}) copy-start(bf16[2,16,32,1024]{3,2,1,0:T(8,128)(2,1)} %get-tuple-element.23.ul_ref) | copy-start | bytes 6291460
  127.8 1.2 copy-start.6
  129.0 8.1 %copy-start.17 = (f32[2,16,16,128]{3,2,1,0:T(8,128)S(1)}, f32[2,16,16,128]{3,2,1,0:T(8,128)}, u32[]{:S(2)}) copy-start(f32[2,16,16,128]{3,2,1,0:T(8,128)} %get-tuple-element.29) | copy-start | bytes 786436

commit v2 on v1

v2 whole, which is shorter than its diff:
```python
import functools
import math

import jax
import jax.numpy as jnp
from jax import lax
from jax.experimental import pallas as pl
from jax.experimental.pallas import tpu as pltpu
from jax.sharding import PartitionSpec as P

MESH = pl.DeviceIdType.MESH
F32 = jnp.float32
BF16 = jnp.bfloat16
NSX = 32
NSY = 8
FORWARD = 1.0 / math.sqrt(128 * 64 * 1024)
INVERSE = 1.0 / math.sqrt(32768)
ROOT_HALF = 1.0 / math.sqrt(2.0)
DENSITY = 1.0 / math.sqrt(2.0 * math.pi)


def iota(shape, dim):
    return lax.broadcasted_iota(jnp.int32, shape, dim)


def split(values):
    high = values.astype(BF16)
    return high, (values - high.astype(F32)).astype(BF16)


def dot(a, b, contract=(1, 0)):
    return lax.dot_general(
        a, b, (((contract[0],), (contract[1],)), ((), ())), preferred_element_type=F32
    )


def dot3(a_high, a_low, b_high, b_low, contract=(1, 0)):
    total = dot(a_high, b_high, contract)
    total += dot(a_high, b_low, contract)
    return total + dot(a_low, b_high, contract)


def mul3(a, b):
    return dot3(*split(a), *split(b))


def turn(phase, length):
    angle = phase.astype(F32) * (2.0 * math.pi / length)
    return jnp.cos(angle), jnp.sin(angle)


def pick(index, mode_ref, count):
    total = jnp.zeros(index.shape, jnp.int32)
    for k in range(count):
        total = jnp.where(index == k, mode_ref[k], total)
    return total


def build_zt(mz_ref, mt_ref, th_ref, tl_ref):
    pair = iota((64, 128), 1)
    cz, sz = turn((iota((64, 128), 0) * pick(pair // 8, mz_ref, 16)) & 63, 64)
    pair = iota((16, 128), 1)
    ct, st = turn((iota((16, 128), 0) * pick(pair % 8, mt_ref, 8)) & 15, 16)
    cz, sz = cz[:, None, :], sz[:, None, :]
    real = (cz * ct - sz * st).reshape(1024, 128)
    imag = (-(sz * ct) - cz * st).reshape(1024, 128)
    th_ref[:, :128], tl_ref[:, :128] = split(real)
    th_ref[:, 128:], tl_ref[:, 128:] = split(imag)


def build_y(my_ref, ty_ref):
    row, col = iota((128, 256), 0), iota((128, 256), 1)
    c, s = turn(((col % 64) * pick(row % 16, my_ref, 16)) & 63, 64)
    same = (row // 64 == col // 128) & ((row // 16) % 2 == (col // 64) % 2)
    ty_ref[...] = jnp.where(same, jnp.where((row // 32) % 2 == 0, c, s), 0.0)


def build_y_back(my_ref, tyi_ref):
    row, col = iota((512, 128), 0), iota((512, 128), 1)
    y = ((row // 32) % 8) * 8 + row % 8
    c, s = turn((y * pick(col % 16, my_ref, 16)) & 63, 64)
    ro, ri = row // 256, (col // 32) % 2
    same = ((row // 8) % 2 == col // 64) & ((row // 16) % 2 == (col // 16) % 2)
    value = jnp.where(ro == ri, c, jnp.where(ro == 0, -s, s))
    tyi_ref[...] = jnp.where(same, value, 0.0)


def build_x(mx_ref, tx_ref):
    row, col = iota((64, 256), 0), iota((64, 256), 1)
    c, s = turn(((col // 2) * pick((row // 8) * 2 + (row // 2) % 2, mx_ref, 16)) & 127, 128)
    ro, ri = row % 2, col % 2
    value = jnp.where(ro == ri, c, jnp.where(ro == 0, s, -s))
    tx_ref[...] = jnp.where(row % 8 < 4, value, 0.0)


def build_x_back(mx_ref, txi_ref):
    row, col = iota((256, 32), 0), iota((256, 32), 1)
    c, s = turn(((row // 2) * pick(col // 2, mx_ref, 16)) & 127, 128)
    ro, ri = row % 2, col % 2
    txi_ref[...] = jnp.where(ro == ri, c, jnp.where(ro == 0, -s, s))


def build_maps(lw_ref, kf_ref, kb_ref):
    row, col = iota((256, 16), 0), iota((256, 16), 1)
    spread = jnp.where(row // 16 == col, 1.0, 0.0)
    high = lax.Precision.HIGHEST
    wide = lax.dot_general(
        spread, lw_ref[...], (((1,), (0,)), ((), ())), precision=high, preferred_element_type=F32
    )
    wide = lax.dot_general(
        wide, spread, (((1,), (1,)), ((), ())), precision=high, preferred_element_type=F32
    )
    row, col = iota((256, 256), 0), iota((256, 256), 1)
    wide = jnp.where(row % 16 == col % 16, wide, 0.0)
    kb_ref[...] = wide
    kf_ref[...] = wide.T


SY_PEERS = ((2, 1), (1, 1), (3, 1), (2, 0), (0, 1), (1, 0), (3, 0))


def swap_lanes(first, second, width):
    low = (iota(first.shape, 1) // width) % 2 == 0
    return (
        jnp.where(low, first, pltpu.roll(second, width, 1)),
        jnp.where(low, pltpu.roll(first, 128 - width, 1), second),
    )


def swap_four(parts):
    a, b, c, d = parts
    a, c = swap_lanes(a, c, 64)
    b, d = swap_lanes(b, d, 64)
    a, b = swap_lanes(a, b, 32)
    c, d = swap_lanes(c, d, 32)
    return a, b, c, d


def gelu_slope(values):
    normal_cdf = 0.5 * (1.0 + lax.erf(values * ROOT_HALF))
    return normal_cdf + values * (jnp.exp(-0.5 * values * values) * DENSITY)


def chain_kernel(
    field_ref, gout_ref, w_hbm, lw_hbm, mx_hbm, my_hbm, mz_hbm, mt_hbm,
    local_out, last_out, th_out, tl_out, gm_out,
    field, gout, fh, fl, sa, ra, sb, rb, sc, rc, sd, rd, ws, wr, turned, spectra, slopes,
    w_ref, lw_ref, th_ref, tl_ref, tx_ref, txi_ref, ty_ref, tyi_ref, kf_ref, kb_ref, gm_ref,
    mx_ref, my_ref, mz_ref, mt_ref,
    load_sem, small_sem, store_sem, sa_send, sa_recv, sa_own, sb_send, sb_recv, sb_own,
    sc_send, sc_recv, sc_own, sd_send, sd_recv, sd_own, w_send, w_recv, w_own,
):
    sx, sy = lax.axis_index("sx"), lax.axis_index("sy")

    def load(b, which):
        source, target = ((field_ref, field), (gout_ref, gout))[which]
        return pltpu.make_async_copy(source.at[b], target.at[b], load_sem.at[which, b])

    def small(i):
        source = (mz_hbm, mt_hbm, mx_hbm, my_hbm, lw_hbm, w_hbm)[i]
        target = (mz_ref, mt_ref, mx_ref, my_ref, lw_ref, w_ref)[i]
        return pltpu.make_async_copy(source, target, small_sem.at[i])

    def store(i):
        source = (gout.at[0], gout.at[1], th_ref, tl_ref, gm_ref)[i]
        target = (local_out.at[0], local_out.at[1], th_out, tl_out, gm_out)[i]
        return pltpu.make_async_copy(source, target, store_sem.at[i])

    small(0).start()
    small(1).start()
    load(0, 0).start()
    barrier = pltpu.get_barrier_semaphore()

    def greet(axis, me, n):
        def one(d, carry):
            pl.semaphore_signal(
                barrier, inc=1, device_id={axis: lax.rem(me + d, n)}, device_id_type=MESH
            )
            return carry

        lax.fori_loop(1, n, one, 0)

    greet("sy", sy, NSY)
    greet("sx", sx, NSX)
    for i in range(2, 6):
        small(i).start()
    load(1, 0).start()
    load(0, 1).start()
    load(1, 1).start()

    def send(axis, to, source, target, sems):
        pltpu.make_async_remote_copy(
            src_ref=source,
            dst_ref=target,
            send_sem=sems[0],
            recv_sem=sems[1],
            device_id={axis: to},
            device_id_type=MESH,
        ).start()

    def over_sy(source, target, sems):
        for dy, dx in SY_PEERS:
            to = lax.rem(sy // 2 + dy, 4) * 2 + lax.rem(sy + dx, 2)
            send("sy", to, source(to), target(sy), sems)
        pltpu.make_async_copy(source(sy), target(sy), sems[2]).start()

    def over_sx(source, target, sems):
        def at(dx, dz, dc):
            to = lax.rem(sx // 16 + dx, 2) * 16 + lax.rem(sx // 2 + dz, 8) * 2 + lax.rem(sx + dc, 2)
            send("sx", to, source(to), target(sx), sems)

        def ring(j, carry):
            dz = 12 + ((j + 1) // 2) * (2 * lax.rem(j, 2) - 1)
            for dx, dc in ((1, 1), (1, 0), (0, 1), (0, 0)):
                at(dx, dz, dc)
            return carry

        lax.fori_loop(0, 7, ring, 0)
        for dx, dc in ((1, 1), (1, 0), (0, 1)):
            at(dx, 0, dc)
        pltpu.make_async_copy(source(sx), target(sx), sems[2]).start()

    def drain(whole, one, sem, own=None):
        pltpu.make_async_copy(whole, whole, sem).wait()
        if own is not None:
            pltpu.make_async_copy(one, one, own).wait()

    def eight(d):
        return pl.ds(pl.multiple_of(d * 8, 8), 8)

    def start_a(k, b):
        target = (lambda d: ra.at[k, b, d]) if k < 3 else (lambda d: last_out.at[b, d])
        over_sy(lambda d: sa.at[k, b, d], target, (sa_send.at[k, b], sa_recv.at[k, b], sa_own.at[k, b]))

    def wait_a(k, b):
        whole = ra.at[k, b] if k < 3 else last_out.at[b]
        drain(whole.at[pl.ds(0, NSY - 1)], whole.at[0], sa_recv.at[k, b], sa_own.at[k, b])

    def start_b(k, b):
        over_sx(
            lambda d: sb.at[k, b, eight(d)],
            lambda d: rb.at[k, b, eight(d)],
            (sb_send.at[k, b], sb_recv.at[k, b], sb_own.at[k, b]),
        )

    def wait_b(k, b):
        whole = rb.at[k, b]
        drain(whole.at[pl.ds(0, (NSX - 1) * 8)], whole.at[pl.ds(0, 8)], sb_recv.at[k, b], sb_own.at[k, b])

    def start_c(k, b):
        over_sy(
            lambda d: sc.at[k, b, eight(d)],
            lambda d: rc.at[k, b, eight(d)],
            (sc_send.at[k, b], sc_recv.at[k, b], sc_own.at[k, b]),
        )

    def wait_c(k, b):
        whole = rc.at[k, b]
        drain(whole.at[pl.ds(0, (NSY - 1) * 8)], whole.at[pl.ds(0, 8)], sc_recv.at[k, b], sc_own.at[k, b])

    def start_d(k, b):
        over_sy(
            lambda d: sd.at[k, b, pl.ds(pl.multiple_of(d * 32, 32), 32)],
            lambda d: rd.at[k, b, d],
            (sd_send.at[k, b], sd_recv.at[k, b], sd_own.at[k, b]),
        )

    def wait_d(k, b):
        whole = rd.at[k, b]
        drain(whole.at[pl.ds(0, NSY - 1)], whole.at[0], sd_recv.at[k, b], sd_own.at[k, b])

    def start_w(k):
        over_sy(lambda d: ws.at[k, d], lambda d: wr.at[k, d], (w_send.at[k], w_recv.at[k], w_own.at[k]))

    def wait_w(k):
        whole = wr.at[k]
        drain(whole.at[pl.ds(0, NSY - 1)], whole.at[0], w_recv.at[k], w_own.at[k])

    def zt_forward(k, b, high_ref, low_ref, source=None):
        def block(m, carry):
            rows = pl.ds(m * 8, 8)
            if source is None:
                high = high_ref[b, rows].reshape(256, 1024)
                low = low_ref[b, rows].reshape(256, 1024)
            else:
                high, low = split(source[b, rows].reshape(256, 1024))
                high_ref[b, rows] = high.reshape(8, 32, 1024)
                low_ref[b, rows] = low.reshape(8, 32, 1024)
            out = dot3(high, low, th_ref[...], tl_ref[...])
            sa[k, b, pl.ds(m * 4, 4)] = out.reshape(4, 64, 256)
            return carry

        lax.fori_loop(0, 2, block, 0)

    def y_forward(ka, kb, b):
        for i in range(2):
            parts = [
                ra[ka, b, :, c * 32 + (i * 2 + x) * 8 : c * 32 + (i * 2 + x) * 8 + 8, :].reshape(64, 256)
                for x in range(2)
                for c in range(2)
            ]
            out = mul3(ty_ref[...], jnp.concatenate(parts, axis=0))
            rows = []
            for x in range(2):
                cos, sin = out[x * 64 : x * 64 + 32], out[x * 64 + 32 : x * 64 + 64]
                rows.append(cos[:, :128] + sin[:, 128:])
                rows.append(cos[:, 128:] - sin[:, :128])
            turned[i] = jnp.concatenate(rows, axis=0).T
            parts = swap_four([turned[i, pl.ds(z, 32, stride=4), :] for z in range(4)])
            for q in range(4):
                sb[kb, b, pl.ds(i * 4 + q, 32, stride=8), :] = parts[q]

    def y_backward(kb, ka, b):
        halves = []
        for i in range(2):
            parts = swap_four([rb[kb, b, pl.ds(i * 4 + q, 32, stride=8), :] for q in range(4)])
            for z in range(4):
                turned[i, pl.ds(z, 32, stride=4), :] = parts[z]
            halves.append(turned[i].T)
        out = mul3(tyi_ref[...], jnp.concatenate(halves, axis=1))
        for part in range(2):
            for i in range(2):
                block = out[part * 256 : part * 256 + 256, i * 128 : i * 128 + 128].reshape(8, 2, 16, 128)
                for o in range(2):
                    sa[ka, b, :, o * 32 + i * 16 : o * 32 + i * 16 + 16, part * 128 : part * 128 + 128] = block[:, o]

    def x_forward(kb, kc, b):
        sc[kc, b] = mul3(tx_ref[...], rb[kb, b])

    def x_backward(kd, kb, b):
        total = rd[kd, b, 0]
        for d in range(1, NSY):
            total += rd[kd, b, d]
        sb[kb, b] = mul3(txi_ref[...], total * (FORWARD * INVERSE))

    def gather_modes(kc, b, keep, factor):
        for part in range(2):
            pair = swap_lanes(
                rc[kc, b, pl.ds(part, 8, stride=8), :], rc[kc, b, pl.ds(2 + part, 8, stride=8), :], 16
            )
            for low in range(2):
                keep[b, part, pl.ds(low, 8, stride=2), :] = pair[low] * factor

    def spread_weights(k):
        inner, outer = (1, 16) if k == 0 else (16, 1)
        for part in range(2):
            for slab in range(NSY):
                for low in range(2):
                    pair = [
                        w_ref[part, pl.ds((slab * 2 + own) * outer + low * inner, 8, stride=2 * inner), :]
                        for own in range(2)
                    ]
                    pair = swap_lanes(pair[0], pair[1], 16)
                    for kx in range(2):
                        ws[k, slab, part, kx, low * 8 : low * 8 + 8, :] = pair[kx]

    def mix(kc, kd, b):
        sign = 1.0 if kd == 0 else -1.0
        low = (iota((8, 128), 1) // 16) % 2 == 0

        def fold(values):
            even, odd = values[:8], values[8:]
            return jnp.where(low, even + pltpu.roll(even, 112, 1), odd + pltpu.roll(odd, 16, 1))

        def line(i, carry):
            for kx in range(2):
                real = sc[kc, b, pl.ds(i * 8 + kx * 2, 1), :]
                imag = sc[kc, b, pl.ds(i * 8 + kx * 2 + 1, 1), :]
                w_real, w_imag = wr[kd, i, 0, kx], wr[kd, i, 1, kx]
                out_real = w_real * real - sign * (w_imag * imag)
                out_imag = w_real * imag + sign * (w_imag * real)
                sd[kd, b, pl.ds(i * 4 + kx * 2, 8, stride=32), :] = fold(out_real)
                sd[kd, b, pl.ds(i * 4 + kx * 2 + 1, 8, stride=32), :] = fold(out_imag)
            return carry

        lax.fori_loop(0, NSY, line, 0, unroll=True)

    def weight_grad():
        for b in range(2):
            wait_c(0, b)
            gather_modes(0, b, spectra, FORWARD)
            wait_c(1, b)
            gather_modes(1, b, slopes, INVERSE)

        def channel(c, carry):
            real = imag = jnp.zeros((16, 128), F32)
            for b in range(2):
                xr, xi = spectra[b, 0, pl.ds(c, 1), :], spectra[b, 1, pl.ds(c, 1), :]
                dr, di = slopes[b, 0], slopes[b, 1]
                real = real + (xr * dr + xi * di)
                imag = imag + (xr * di - xi * dr)
            gm_ref[0, c] = real
            gm_ref[1, c] = imag
            return carry

        lax.fori_loop(0, 16, channel, 0)

    def channel_map(b, k_ref, high_ref, low_ref, target):
        kh, kl = split(k_ref[...])
        for g in range(2):
            cells = slice(g * 16, g * 16 + 16)

            def columns(n, carry):
                cols = pl.ds(pl.multiple_of(n * 256, 256), 256)
                out = dot3(
                    kh,
                    kl,
                    high_ref[b, :, cells, cols].reshape(256, 256),
                    low_ref[b, :, cells, cols].reshape(256, 256),
                )
                target[b, :, cells, cols] = out.reshape(16, 16, 256)
                return carry

            lax.fori_loop(0, 4, columns, 0, unroll=True)

    def slope_stage(ka, b):
        for g in range(2):
            cells = slice(g * 16, g * 16 + 16)
            parts = [ra[ka, b, :, o * 32 + g * 16 : o * 32 + g * 16 + 16, :] for o in range(2)]
            lh, ll = split(jnp.concatenate(parts, axis=1).reshape(256, 256))

            def columns(n, carry):
                cols = pl.ds(pl.multiple_of(n * 256, 256), 256)
                hidden = dot3(lh, ll, th_ref[cols, :], tl_ref[cols, :], (1, 1))
                hidden += field[b, :, cells, cols].reshape(256, 256)
                upstream = gout[b, :, cells, cols].reshape(256, 256) * gelu_slope(hidden)
                high, low = split(upstream)
                fh[b, :, cells, cols] = high.reshape(16, 16, 256)
                fl[b, :, cells, cols] = low.reshape(16, 16, 256)
                return carry

            lax.fori_loop(0, 4, columns, 0, unroll=True)

    small(0).wait()
    small(1).wait()
    build_zt(mz_ref, mt_ref, th_ref, tl_ref)
    store(2).start()
    store(3).start()
    load(0, 0).wait()
    zt_forward(0, 0, fh, fl, field)
    pl.semaphore_wait(barrier, NSX + NSY - 2)
    start_a(0, 0)
    load(1, 0).wait()
    zt_forward(0, 1, fh, fl, field)
    for i in range(2, 6):
        small(i).wait()
    spread_weights(0)
    start_w(0)
    start_a(0, 1)
    build_y(my_ref, ty_ref)
    build_x(mx_ref, tx_ref)
    build_maps(lw_ref, kf_ref, kb_ref)
    build_x_back(mx_ref, txi_ref)
    build_y_back(my_ref, tyi_ref)
    spread_weights(1)

    def map_field(b):
        channel_map(b, kf_ref, fh, fl, field)

    def map_upstream(b):
        channel_map(b, kb_ref, fh, fl, gout)
        store(b).start()

    def there_and_back(k, aside):
        ka = kb = 2 * k
        wait_a(ka, 0)
        y_forward(ka, kb, 0)
        start_b(kb, 0)
        aside(0)
        wait_b(kb, 0)
        x_forward(kb, k, 0)
        if k == 0:
            wait_w(0)
        mix(k, k, 0)
        start_d(k, 0)
        start_c(k, 0)
        wait_a(ka, 1)
        y_forward(ka, kb, 1)
        start_b(kb, 1)
        if k == 0:
            start_w(1)
        wait_d(k, 0)
        x_backward(k, kb + 1, 0)
        start_b(kb + 1, 0)
        wait_b(kb, 1)
        x_forward(kb, k, 1)
        mix(k, k, 1)
        start_d(k, 1)
        start_c(k, 1)
        aside(1)
        wait_d(k, 1)
        x_backward(k, kb + 1, 1)
        start_b(kb + 1, 1)
        wait_b(kb + 1, 0)
        y_backward(kb + 1, ka + 1, 0)
        start_a(ka + 1, 0)
        if k == 1:
            weight_grad()
            store(4).start()
        wait_b(kb + 1, 1)
        y_backward(kb + 1, ka + 1, 1)
        start_a(ka + 1, 1)
        wait_a(ka + 1, 0)

    there_and_back(0, map_field)
    load(0, 1).wait()
    slope_stage(1, 0)
    zt_forward(2, 0, fh, fl)
    start_a(2, 0)
    wait_w(1)
    wait_a(1, 1)
    load(1, 1).wait()
    slope_stage(1, 1)
    zt_forward(2, 1, fh, fl)
    start_a(2, 1)
    there_and_back(1, map_upstream)
    for k in range(2):
        drain(ws.at[k, pl.ds(0, NSY - 1)], None, w_send.at[k])
        for b in range(2):
            drain(sc.at[k, b, pl.ds(0, (NSY - 1) * 8)], None, sc_send.at[k, b])
            drain(sd.at[k, b, pl.ds(0, (NSY - 1) * 32)], None, sd_send.at[k, b])
    for k in range(4):
        for b in range(2):
            drain(sb.at[k, b, pl.ds(0, (NSX - 1) * 8)], None, sb_send.at[k, b])
            drain(sa.at[k, b, pl.ds(0, NSY - 1)], None, sa_send.at[k, b])
    for i in range(5):
        store(i).wait()
    wait_a(3, 1)


def chain(field, gout, weight, local_weight, mode_x, mode_y, mode_z, mode_t):
    shape = jax.ShapeDtypeStruct
    any_space = pl.BlockSpec(memory_space=pl.ANY)
    sems = pltpu.SemaphoreType.DMA
    vmem, smem = pltpu.VMEM, pltpu.SMEM
    return pl.pallas_call(
        chain_kernel,
        out_shape=(
            shape((2, 16, 32, 1024), F32),
            shape((2, 8, 64, 256), F32),
            shape((1024, 256), BF16),
            shape((1024, 256), BF16),
            shape((2, 16, 16, 128), F32),
        ),
        in_specs=[any_space] * 8,
        out_specs=[any_space] * 5,
        scratch_shapes=[
            vmem((2, 16, 32, 1024), F32),
            vmem((2, 16, 32, 1024), F32),
            vmem((2, 16, 32, 1024), BF16),
            vmem((2, 16, 32, 1024), BF16),
            vmem((4, 2, 8, 64, 256), F32),
            vmem((3, 2, 8, 64, 256), F32),
            vmem((4, 2, 256, 128), F32),
            vmem((4, 2, 256, 128), F32),
            vmem((2, 2, 64, 128), F32),
            vmem((2, 2, 64, 128), F32),
            vmem((2, 2, 256, 128), F32),
            vmem((2, 2, 8, 32, 128), F32),
            vmem((2, 8, 2, 2, 16, 128), F32),
            vmem((2, 8, 2, 2, 16, 128), F32),
            vmem((2, 128, 128), F32),
            vmem((2, 2, 16, 128), F32),
            vmem((2, 2, 16, 128), F32),
            vmem((2, 256, 128), F32),
            vmem((16, 16), F32),
            vmem((1024, 256), BF16),
            vmem((1024, 256), BF16),
            vmem((64, 256), F32),
            vmem((256, 32), F32),
            vmem((128, 256), F32),
            vmem((512, 128), F32),
            vmem((256, 256), F32),
            vmem((256, 256), F32),
            vmem((2, 16, 16, 128), F32),
            smem((16,), jnp.int32),
            smem((16,), jnp.int32),
            smem((16,), jnp.int32),
            smem((8,), jnp.int32),
            sems((2, 2)),
            sems((6,)),
            sems((5,)),
        ]
        + [sems((4, 2))] * 6
        + [sems((2, 2))] * 6
        + [sems((2,))] * 3,
        compiler_params=pltpu.CompilerParams(
            collective_id=1, has_side_effects=True, vmem_limit_bytes=56 << 20
        ),
        name="chain",
    )(field, gout, weight, local_weight, mode_x, mode_y, mode_z, mode_t)


def finish_kernel(spectra_ref, local_ref, th_ref, tl_ref, gm_ref, out_ref, gm_out):
    gm_out[...] = gm_ref[...]
    parts = [spectra_ref[0, :, o, :, :] for o in range(2)]
    lh, ll = split(jnp.concatenate(parts, axis=1).reshape(256, 256))

    def columns(n, carry):
        cols = pl.ds(pl.multiple_of(n * 256, 256), 256)
        total = dot3(lh, ll, th_ref[cols, :], tl_ref[cols, :], (1, 1))
        out_ref[0, :, :, cols] = total.reshape(16, 16, 256) + local_ref[0, :, :, cols]
        return carry

    lax.fori_loop(0, 4, columns, 0, unroll=True)


def finish(spectra, local, th, tl, grad_modes):
    cells = pl.BlockSpec((1, 16, 16, 1024), lambda b, g: (b, 0, g, 0))
    table = pl.BlockSpec((1024, 256), lambda b, g: (0, 0))
    modes = pl.BlockSpec((1, 16, 16, 128), lambda b, g: (b, 0, 0, 0))
    return pl.pallas_call(
        finish_kernel,
        grid=(2, 2),
        out_shape=(
            jax.ShapeDtypeStruct((2, 16, 32, 1024), F32),
            jax.ShapeDtypeStruct((2, 16, 16, 128), F32),
        ),
        in_specs=[
            pl.BlockSpec((1, 8, 2, 16, 256), lambda b, g: (b, 0, 0, g, 0)),
            cells,
            table,
            table,
            modes,
        ],
        out_specs=(cells, modes),
        compiler_params=pltpu.CompilerParams(vmem_limit_bytes=60 << 20),
        name="finish",
    )(spectra.reshape(2, 8, 2, 32, 256), local, th, tl, grad_modes)


def body(field, grad_out, local_weight, mode_weight, mode_x, mode_y, mode_z, mode_t):
    local, spectra, th, tl, grad_modes = chain(
        field.reshape(2, 16, 32, 1024),
        grad_out.reshape(2, 16, 32, 1024),
        mode_weight.reshape(2, 256, 128),
        local_weight,
        mode_x,
        mode_y,
        mode_z,
        mode_t,
    )
    grad_input, grad_modes = finish(spectra, local, th, tl, grad_modes)
    return grad_input.reshape(field.shape), grad_modes


def solution(mesh):
    grid = P(None, None, "sx", "sy", None)
    modes = P(None, None, None, ("sx", "sy"))
    return jax.shard_map(
        body,
        mesh=mesh,
        in_specs=(grid, grid, P(), modes, P(), P(), P(), P()),
        out_specs=(grid, modes),
        check_vma=False,
    )
```

time: 138 us -> 105 us (0.76)
  Pallas kernels: 124 us -> 104 us
  local copies, waits for them, and re-layouts: 13.4 us -> 0 us
    pallas_call x3 -> x2, Pallas kernels: 124 us -> 104 us  [the longest x1 97.3 us: chain(): pl.pallas_call(chain_kernel, out_shape=(shape((2, 16, 32, 1024), F32), sh...]
    unnamed x37 -> x0, local copies, waits for them, and re-layouts: 13.4 us -> none
where the time goes in v2:
time: 105 us
  Pallas kernels  104 us (99%)
    pallas_call x1, Pallas kernels, chain(): pl.pallas_call(chain_kernel, out_shape=(shape((2, 16, 32, 1024), F32), sh...  97.3 us
    pallas_call x1, Pallas kernels, finish(): pl.pallas_call(finish_kernel, grid=(2, 2), out_shape=(jax.ShapeDtypeStruc...  6.6 us

profile of v2, /device:TPU:1, one launch (start us, length us, event | category | flops | bytes accessed | tf_op | source)
XLA Modules:
  0.0 104.5 jit_solution(7653512408705268075)
XLA Ops:
  0.6 97.3 %chain.1 = (f32[2,16,32,1024]{3,2,1,0:T(8,128)}, f32[2,8,64,256]{3,2,1,0:T(8,128)}, bf16[1024,256]{1,0:T(8,128)(2,1)}, bf16[1024,256]{1,0:T(8,128)(2,1)}, f32[2,16,16,128]{3,2,1,0:T(8,128)}) custom-call(f32[2,16,32,1024]{3,2,1,0:T(8,128)} %bitcast.5, f32[2,16,32,1024]{3,2,1,0:T(8,128)} %bitcast.6, f32[2,256,128]{2,1,0:T(8,128)} %bitcast.8, f32[16,16]{1,0:T(8,128)} %lw_hbm.1, ...), custom_call_target="tpu_custom_call" | custom-call | tf_op jit(solution)/shard_map/chain/pallas_call | solution.py:536
  97.9 6.6 %finish.1 = (f32[2,16,32,1024]{3,2,1,0:T(8,128)}, f32[2,16,16,128]{3,2,1,0:T(8,128)}) custom-call(f32[2,8,2,32,256]{4,3,2,1,0:T(8,128)} %bitcast.7, f32[2,16,32,1024]{3,2,1,0:T(8,128)} %get-tuple-element.10.local_ref, bf16[1024,256]{1,0:T(8,128)(2,1)} %get-tuple-element.11.th_ref, bf16[1024,256]{1,0:T(8,128)(2,1)} %get-tuple-element.12.tl_ref, ...), custom_call_target="tpu_custom_call" | custom-call | tf_op jit(solution)/shard_map/finish/pallas_call | solution.py:612

commit v3 on v2

--- a/solution.py
+++ b/solution.py
@@ -591,39 +591,68 @@
     )(field, gout, weight, local_weight, mode_x, mode_y, mode_z, mode_t)
 
 
-def finish_kernel(spectra_ref, local_ref, th_ref, tl_ref, gm_ref, out_ref, gm_out):
-    gm_out[...] = gm_ref[...]
-    parts = [spectra_ref[0, :, o, :, :] for o in range(2)]
-    lh, ll = split(jnp.concatenate(parts, axis=1).reshape(256, 256))
-
-    def columns(n, carry):
-        cols = pl.ds(pl.multiple_of(n * 256, 256), 256)
-        total = dot3(lh, ll, th_ref[cols, :], tl_ref[cols, :], (1, 1))
-        out_ref[0, :, :, cols] = total.reshape(16, 16, 256) + local_ref[0, :, :, cols]
-        return carry
-
-    lax.fori_loop(0, 4, columns, 0, unroll=True)
+def finish_kernel(
+    spectra_hbm, local_hbm, th_hbm, tl_hbm, gm_hbm, out_hbm, gm_out, spectra, local, th, tl, gm, load_sem, store_sem
+):
+    def load(i):
+        source = (th_hbm, tl_hbm, spectra_hbm.at[0], spectra_hbm.at[1], gm_hbm)[i]
+        target = (th, tl, spectra.at[0], spectra.at[1], gm)[i]
+        return pltpu.make_async_copy(source, target, load_sem.at[i])
+
+    def part(hbm, b, g, sem, out):
+        rows = (b, slice(None), pl.ds(g * 16, 16))
+        pair = (local.at[rows], hbm.at[rows]) if out else (hbm.at[rows], local.at[rows])
+        return pltpu.make_async_copy(*pair, sem)
+
+    order = [(b, g) for b in range(2) for g in range(2)]
+    for i in range(3):
+        load(i).start()
+    for i, (b, g) in enumerate(order):
+        part(local_hbm, b, g, load_sem.at[5 + i], False).start()
+        if i == 0:
+            load(3).start()
+    load(4).start()
+    load(0).wait()
+    load(1).wait()
+    for i, (b, g) in enumerate(order):
+        if g == 0:
+            load(2 + b).wait()
+        lh, ll = split(jnp.concatenate([spectra[b, :, o, g * 16 : g * 16 + 16, :] for o in range(2)], axis=1).reshape(256, 256))
+        part(local_hbm, b, g, load_sem.at[5 + i], False).wait()
+        cells = slice(g * 16, g * 16 + 16)
+        for n in range(4):
+            cols = slice(n * 256, n * 256 + 256)
+            total = dot3(lh, ll, th[cols, :], tl[cols, :], (1, 1))
+            local[b, :, cells, cols] = total.reshape(16, 16, 256) + local[b, :, cells, cols]
+        part(out_hbm, b, g, store_sem.at[i], True).start()
+        if i == 0:
+            load(4).wait()
+            pltpu.make_async_copy(gm, gm_out, store_sem.at[4]).start()
+    for i, (b, g) in enumerate(order):
+        part(out_hbm, b, g, store_sem.at[i], True).wait()
+    pltpu.make_async_copy(gm, gm_out, store_sem.at[4]).wait()
 
 
 def finish(spectra, local, th, tl, grad_modes):
-    cells = pl.BlockSpec((1, 16, 16, 1024), lambda b, g: (b, 0, g, 0))
-    table = pl.BlockSpec((1024, 256), lambda b, g: (0, 0))
-    modes = pl.BlockSpec((1, 16, 16, 128), lambda b, g: (b, 0, 0, 0))
+    any_space = pl.BlockSpec(memory_space=pl.ANY)
+    vmem = pltpu.VMEM
     return pl.pallas_call(
         finish_kernel,
-        grid=(2, 2),
         out_shape=(
             jax.ShapeDtypeStruct((2, 16, 32, 1024), F32),
             jax.ShapeDtypeStruct((2, 16, 16, 128), F32),
         ),
-        in_specs=[
-            pl.BlockSpec((1, 8, 2, 16, 256), lambda b, g: (b, 0, 0, g, 0)),
-            cells,
-            table,
-            table,
-            modes,
+        in_specs=[any_space] * 5,
+        out_specs=(any_space, any_space),
+        scratch_shapes=[
+            vmem((2, 8, 2, 32, 256), F32),
+            vmem((2, 16, 32, 1024), F32),
+            vmem((1024, 256), BF16),
+            vmem((1024, 256), BF16),
+            vmem((2, 16, 16, 128), F32),
+            pltpu.SemaphoreType.DMA((9,)),
+            pltpu.SemaphoreType.DMA((5,)),
         ],
-        out_specs=(cells, modes),
         compiler_params=pltpu.CompilerParams(vmem_limit_bytes=60 << 20),
         name="finish",
     )(spectra.reshape(2, 8, 2, 32, 256), local, th, tl, grad_modes)

time: 105 us -> 104 us (level)
  no operation moved by 1% of the time
where the time goes in v3:
time: 104 us
  Pallas kernels  103 us (99%)
    pallas_call x1, Pallas kernels, chain(): pl.pallas_call(chain_kernel, out_shape=(shape((2, 16, 32, 1024), F32), sh...  97.3 us
    pallas_call x1, Pallas kernels, finish(): pl.pallas_call(finish_kernel, out_shape=(jax.ShapeDtypeStruct((2, 16, 32,...  5.84 us

profile of v3, /device:TPU:1, one launch (start us, length us, event | category | flops | bytes accessed | tf_op | source)
XLA Modules:
  0.0 103.9 jit_solution(1015948559859697423)
XLA Ops:
  0.6 97.3 %chain.1 = (f32[2,16,32,1024]{3,2,1,0:T(8,128)}, f32[2,8,64,256]{3,2,1,0:T(8,128)}, bf16[1024,256]{1,0:T(8,128)(2,1)}, bf16[1024,256]{1,0:T(8,128)(2,1)}, f32[2,16,16,128]{3,2,1,0:T(8,128)}) custom-call(f32[2,16,32,1024]{3,2,1,0:T(8,128)} %bitcast.5, f32[2,16,32,1024]{3,2,1,0:T(8,128)} %bitcast.6, f32[2,256,128]{2,1,0:T(8,128)} %bitcast.8, f32[16,16]{1,0:T(8,128)} %lw_hbm.1, ...), custom_call_target="tpu_custom_call" | custom-call | tf_op jit(solution)/shard_map/chain/pallas_call | solution.py:536
  97.9 5.8 %finish.1 = (f32[2,16,32,1024]{3,2,1,0:T(8,128)}, f32[2,16,16,128]{3,2,1,0:T(8,128)}) custom-call(f32[2,8,2,32,256]{4,3,2,1,0:T(8,128)} %bitcast.7, f32[2,16,32,1024]{3,2,1,0:T(8,128)} %get-tuple-element.10.local_hbm, bf16[1024,256]{1,0:T(8,128)(2,1)} %get-tuple-element.11.th_hbm, bf16[1024,256]{1,0:T(8,128)(2,1)} %get-tuple-element.12.tl_hbm, ...), custom_call_target="tpu_custom_call" | custom-call | tf_op jit(solution)/shard_map/finish/pallas_call | solution.py:639
